TPU v7x, 32 devices: a whole 2x2x4 slice. The times are simulated.
32 devices in a mesh: grp: 2 (over y), term: 4 (over z), batch: 2 (over x), sub: 2 (over core).
Axes of the slice: x: 2, y: 2, z: 4, core: 2. Of those that a mesh axis runs over, the one named last changes fastest.
Arguments:
- query_logits: bfloat16 [256, 151936], P(('grp', 'batch', 'sub'), 'term'), parts along dimension 0, may hold values from -8 to 8
- doc_logits: bfloat16 [1024, 151936], P(('grp', 'batch', 'sub'), 'term'), parts along dimension 0, may hold values from -8 to 8
- score_grad: bfloat16 [256, 512], P(('grp', 'term'), ('batch', 'sub')), parts along dimension 0, may hold values from -0.3984375 to 0.3984375
Outputs:
- query_logit_grad: bfloat16 [256, 151936], P(('grp', 'batch', 'sub'), 'term'), parts along dimension 0
- doc_logit_grad: bfloat16 [1024, 151936], P(('grp', 'batch', 'sub'), 'term'), parts along dimension 0
There are 2 independent parts, one for each index of `grp`. A program takes and returns all parts, laid end to end along the dimension named above; each array names one. Nothing has to cross between parts.
All inputs are finite; a program needn't handle non-finite values.
Results may differ from a plain program's by a relative error of at most 0.01.
Values may be sent and summed in bfloat16 or wider, within the bound.
A program may use at most 192 MiB of HBM per device.

v0:
```python
import jax
import jax.numpy as jnp
from jax import lax
from jax.sharding import PartitionSpec as P

query_reg = 1.0
doc_reg = 0.6


def impacts(logits):
    return jnp.log1p(jnp.maximum(logits.astype(jnp.float32), 0.0)).astype(jnp.bfloat16)


def saturate_back(grad, logits):
    values = logits.astype(jnp.float32)
    scaled = grad / (1.0 + jnp.maximum(values, 0.0))
    return jnp.where(values > 0.0, scaled, 0.0).astype(jnp.bfloat16)


def on_device(query_logits, doc_logits, score_grad):
    group_size = lax.axis_size(("batch", "sub"))
    score_cols = lax.all_gather(score_grad, "term", axis=0, tiled=True)
    query_impact = impacts(query_logits)
    doc_impact = impacts(doc_logits)
    query_rows = query_impact.shape[0]
    doc_rows = doc_impact.shape[0]
    local_sums = (
        jnp.sum(query_impact, axis=0, dtype=jnp.float32),
        jnp.sum(doc_impact, axis=0, dtype=jnp.float32),
    )
    query_sums, doc_sums = lax.psum((local_sums[0], local_sums[1]), ("batch", "sub"))
    grad_rows = score_cols
    doc_grad = lax.dot_general(
        grad_rows,
        lax.all_gather(query_impact, ("batch", "sub"), axis=0, tiled=True),
        (((0,), (0,)), ((), ())),
        preferred_element_type=jnp.float32,
    )
    grad_rows = score_cols
    query_grad = lax.psum_scatter(
        jnp.dot(grad_rows, doc_impact, preferred_element_type=jnp.float32).astype(jnp.bfloat16),
        ("batch", "sub"),
        scatter_dimension=0,
        tiled=True,
    ).astype(jnp.float32)
    query_mean = query_sums / (query_rows * group_size)
    doc_mean = doc_sums / (doc_rows * group_size)
    query_grad = query_grad + 2.0 * query_reg * query_mean[None, :]
    doc_grad = doc_grad + 2.0 * doc_reg * doc_mean[None, :]
    return (saturate_back(query_grad, query_logits), saturate_back(doc_grad, doc_logits))


def solution(mesh):
    placed = (
        P(("grp", "batch", "sub"), "term"),
        P(("grp", "batch", "sub"), "term"),
        P(("grp", "term"), ("batch", "sub")),
    )
    return jax.shard_map(
        on_device,
        mesh=mesh,
        in_specs=placed,
        out_specs=(P(("grp", "batch", "sub"), "term"), P(("grp", "batch", "sub"), "term")),
        check_vma=False,
    )
```

profile of v0, /device:TPU:0, one launch (start us, length us, event | category | flops | bytes accessed | tf_op | source)
XLA Modules:
  0.0 220.8 jit_solution(8904082635508339269)
XLA Ops:
  7.2 0.0 copy-start.1
  7.2 0.0 all-reduce.3.cloned.1.call-start
  7.2 5.7 %fusion.11 = (bf16[32,37984]{1,0:T(8,128)(2,1)}, f32[37984]{0:T(1024)}) fusion(bf16[32,37984]{1,0:T(8,128)(2,1)} %param.3), kind=kLoop, calls=%fused_computation.17 | loop fusion | flops 6039456 | bytes 5013888 | tf_op jit(solution)/shard_map/convert_element_type | solution.py:11
  12.9 10.4 %convert_reduce_fusion = f32[37984]{0:T(1024)} fusion(bf16[128,37984]{0,1:T(8,128)(2,1)} %param.4), kind=kLoop, calls=%fused_computation.12 | loop fusion | flops 24271776 | bytes 9875840 | tf_op jit(solution)/shard_map/reduce_sum | solution.py:29
  23.3 0.0 all-reduce.3.cloned.1.call-update
  23.4 0.0 all-gather.2.cloned.1.call-start
  23.4 0.7 all-gather.2.cloned.1.call-update
  24.1 0.0 reduce-scatter.4.cloned.1.call-start
  24.2 0.0 copy-done.1
  24.2 15.0 %all_gather.6 = bf16[128,128]{1,0:T(8,128)(2,1)S(1)} all-gather(bf16[32,128]{1,0:T(8,128)(2,1)S(1)} %copy-done.1), channel_id=1, replica_groups=mesh['grp'=2,'term'=4,'batch'=2,'sub'=2] {'term'}, dimensions={0}, use_global_device_ids=true | all-gather | bytes 40960 | tf_op jit(solution)/shard_map/all_gather | solution.py:22
  39.2 12.5 %fusion.1 = bf16[128,37984]{0,1:T(8,128)(2,1)} fusion(bf16[128,128]{1,0:T(8,128)(2,1)S(1)} %all_gather.6, bf16[128,37984]{0,1:T(8,128)(2,1)} %param.4), kind=kOutput, calls=%fused_computation.3 | convolution fusion | flops 1264107520 | bytes 19480576 | tf_op jit(solution)/shard_map/dot_general | solution.py:41
  51.7 13.0 %copy.11 = bf16[128,37984]{1,0:T(8,128)(2,1)} copy(bf16[128,37984]{0,1:T(8,128)(2,1)} %fusion.1) | data formatting | bytes 19447808
  64.7 0.0 reduce-scatter.4.cloned.1.call-update
  64.7 0.0 all-reduce.3.cloned.1.call-done
  64.8 1.0 broadcast_multiply_fusion
  65.8 61.0 %all-gather.2.cloned.1.call-done = bf16[128,37984]{1,0:T(8,128)(2,1)} async-done(((bf16[32,37984]{1,0:T(8,128)(2,1)}), bf16[128,37984]{1,0:T(8,128)(2,1)}) %all-gather.2.cloned.1.call-update) | async-done | bytes 9723920 | tf_op jit(solution)/shard_map/all_gather | solution.py:35
  126.8 0.0 copy-start
  126.8 21.5 %fusion.4 = bf16[128,37984]{0,1:T(8,128)(2,1)} fusion(bf16[128,37984]{1,0:T(8,128)(2,1)} %all-gather.2.cloned.1.call-done, bf16[128,128]{1,0:T(8,128)(2,1)S(1)} %all_gather.6, bf16[128,37984]{0,1:T(8,128)(2,1)} %param.4, f32[37984]{0:T(1024)S(1)} %get-tuple-element.10), kind=kOutput, calls=%fused_computation.6 | convolution fusion | flops 1283555328 | bytes 29356416 | tf_op jit(solution)/shard_map/dot_general | solution.py:33
  148.3 61.4 %reduce-scatter.4.cloned.1.call-done = bf16[32,37984]{1,0:T(8,128)(2,1)} async-done(((bf16[128,37984]{1,0:T(8,128)(2,1)}), bf16[32,37984]{1,0:T(8,128)(2,1)}) %reduce-scatter.4.cloned.1.call-update) | async-done | bytes 2430992 | tf_op jit(solution)/shard_map/reduce_scatter | solution.py:40
  209.7 0.0 copy-done
  209.7 4.6 %fusion.14 = bf16[32,37984]{1,0:T(8,128)(2,1)} fusion(bf16[32,37984]{1,0:T(8,128)(2,1)S(1)} %copy-done, bf16[32,37984]{1,0:T(8,128)(2,1)} %reduce-scatter.4.cloned.1.call-done, f32[37984]{0:T(1024)S(1)} %get-tuple-element.11), kind=kLoop, calls=%fused_computation.21 | loop fusion | flops 10939392 | bytes 7444864 | tf_op jit(solution)/shard_map/convert_element_type | solution.py:17
Async XLA Ops:
  7.2 17.0 %copy-start.1 = (bf16[32,128]{1,0:T(8,128)(2,1)S(1)}, bf16[32,128]{1,0:T(8,128)(2,1)}, u32[]{:S(2)}) copy-start(bf16[32,128]{1,0:T(8,128)(2,1)} %param.5) | copy-start | bytes 24580
  7.2 57.6 %all-reduce.3.cloned.1.call-start = ((), (), s32[]{:S(2)}) async-start(), calls=%async_computation.3 | async-start | bytes 622592 | tf_op jit(solution)/shard_map/psum | solution.py:31
  23.4 103.4 %all-gather.2.cloned.1.call-start = ((), (), s32[]{:S(2)}) async-start(), calls=%async_computation.1 | async-start | bytes 12165120 | tf_op jit(solution)/shard_map/all_gather | solution.py:35
  24.1 185.6 %reduce-scatter.4.cloned.1.call-start = ((), (), s32[]{:S(2)}) async-start(), calls=%async_computation.2 | async-start | bytes 12165120 | tf_op jit(solution)/shard_map/reduce_scatter | solution.py:40
  126.8 82.9 %copy-start = (bf16[32,37984]{1,0:T(8,128)(2,1)S(1)}, bf16[32,37984]{1,0:T(8,128)(2,1)}, u32[]{:S(2)}) copy-start(bf16[32,37984]{1,0:T(8,128)(2,1)} %param.3) | copy-start | bytes 7292932
Sparse Core Ops, SparseCore 0:
  23.5 34.7 all-reduce.2
  60.4 66.2 all-gather.1
  129.4 80.2 reduce-scatter.3
where the time goes:
time: 221 us
  waiting for transfers between devices  123 us (56%)
  matrix products  34.1 us (15%)
  other arithmetic  21.8 us (10%)
  blocking collectives  15 us (7%)
  between operations  13.8 us (6%)
  local copies, waits for them, and re-layouts  13 us (6%)
    reduce_scatter x1, waiting for transfers between devices, on_device(): lax.psum_scatter(jnp.dot(grad_rows, doc_impact, preferred_element_type=jn...  61.4 us
    all_gather x1, waiting for transfers between devices, on_device(): lax.all_gather(query_impact, ('batch', 'sub'), axis=0, tiled=True)  61 us
    dot_general x1, matrix products, on_device(): lax.dot_general(grad_rows, lax.all_gather(query_impact, ('batch', 'sub'),...  21.5 us
    all_gather x1, blocking collectives, on_device(): score_cols = lax.all_gather(score_grad, 'term', axis=0, tiled=True)  15 us
    unnamed x5, local copies, waits for them, and re-layouts  13 us
    dot_general x1, matrix products, on_device(): jnp.dot(grad_rows, doc_impact, preferred_element_type=jnp.float32)  12.5 us
    reduce_sum x1, other arithmetic, on_device(): jnp.sum(doc_impact, axis=0, dtype=jnp.float32)  10.4 us
    convert_element_type x1, other arithmetic, impacts(): jnp.log1p(jnp.maximum(logits.astype(jnp.float32), 0.0)).astype(jnp.bfloat16)  5.72 us
  transfers between devices with their start and end apart: 3, of which 2 were waited for; matrix products, arithmetic and copies ran while one was open for 22% of the time, Pallas kernels for 0%

commit v1 on v0

v1 whole, which is shorter than its diff:
```python
import functools

import jax
import jax.numpy as jnp
from jax import lax
from jax.experimental import pallas as pl
from jax.experimental.pallas import tpu as pltpu
from jax.sharding import PartitionSpec as P

query_reg = 1.0
doc_reg = 0.6

LANES = 128
CHUNK_TILES = 11
FORWARD_LAG = 2
OUT_LAG = 3
MESH = pl.DeviceIdType.MESH


def impacts(logits):
    return jnp.log1p(jnp.maximum(logits.astype(jnp.float32), 0.0)).astype(jnp.bfloat16)


def saturate_back(grad, logits):
    values = logits.astype(jnp.float32)
    scaled = grad / (1.0 + jnp.maximum(values, 0.0))
    return jnp.where(values > 0.0, scaled, 0.0).astype(jnp.bfloat16)


def kernel(
    chips, terms, chunks, num_queries, num_docs,
    score_ref, q_in, d_in, q_again, d_again, q_out, d_out,
    score_all, score_keep_send, score_t,
    q_all, p_keep, p_send, p_recv, x_send, x_recv, s_own, s_recv, s_chip, s_far,
    sc_ss, sc_rs, qs_ss, qs_rs, qx_ss, qx_rs, qf_ss, qf_rs,
    p_ss, p_rs, x_ss, x_rs, s_ss, s_rs, sx_ss, sx_rs,
):
    step = pl.program_id(0)
    rows = q_in.shape[0]
    term = lax.axis_index("term")
    chip = lax.axis_index("batch")
    core = lax.axis_index("sub")
    other = 1 - core
    sibling = {"sub": other}
    block = chip * 2 + core

    def chip_up(k):
        return lax.rem(chip + k, chips)

    def chip_down(k):
        return lax.rem(chip + chips - k, chips)

    def remote(src, dst, send, recv, device):
        return pltpu.make_async_remote_copy(
            src_ref=src, dst_ref=dst, send_sem=send, recv_sem=recv,
            device_id=device, device_id_type=MESH,
        )

    def score_copy(k):
        return remote(
            score_all.at[term], score_all.at[term], sc_ss.at[k - 1], sc_rs.at[k - 1],
            {"term": lax.rem(term + k, terms)},
        )

    def score_arrival(k):
        source = lax.rem(term + terms - k, terms)
        return remote(
            score_all.at[source], score_all.at[source], sc_ss.at[k - 1], sc_rs.at[k - 1],
            {"term": lax.rem(term + k, terms)},
        )

    def q_to_sibling(c):
        return remote(q_all.at[c, block], q_all.at[c, block], qs_ss.at[c], qs_rs.at[c], sibling)

    def q_from_sibling(c):
        at = chip * 2 + other
        return remote(q_all.at[c, at], q_all.at[c, at], qs_ss.at[c], qs_rs.at[c], sibling)

    def q_to_chip(c, k):
        return remote(
            q_all.at[c, block], q_all.at[c, block], qx_ss.at[c, k - 1], qx_rs.at[c, k - 1],
            {"batch": chip_up(k)},
        )

    def q_from_chip(c, k):
        at = chip_down(k) * 2 + core
        return remote(
            q_all.at[c, at], q_all.at[c, at], qx_ss.at[c, k - 1], qx_rs.at[c, k - 1],
            {"batch": chip_up(k)},
        )

    def q_forward(c, k):
        at = chip_down(k) * 2 + core
        return remote(
            q_all.at[c, at], q_all.at[c, at], qf_ss.at[c, k - 1], qf_rs.at[c, k - 1], sibling
        )

    def q_forwarded(c, k):
        at = chip_down(k) * 2 + other
        return remote(
            q_all.at[c, at], q_all.at[c, at], qf_ss.at[c, k - 1], qf_rs.at[c, k - 1], sibling
        )

    def p_copy(c):
        return remote(p_send.at[c], p_recv.at[c], p_ss.at[c], p_rs.at[c], sibling)

    def x_copy(c, k):
        return remote(
            x_send.at[c, k - 1], x_recv.at[c, k - 1], x_ss.at[c, k - 1], x_rs.at[c, k - 1],
            {"batch": chip_up(k)},
        )

    def s_copy(c):
        return remote(s_own.at[c], s_recv.at[c], s_ss.at[c], s_rs.at[c], sibling)

    def sx_copy(c, k):
        return remote(
            s_chip.at[c], s_far.at[c, k - 1], sx_ss.at[c, k - 1], sx_rs.at[c, k - 1],
            {"batch": chip_up(k)},
        )

    @pl.when(step == 0)
    def _():
        barrier = pltpu.get_barrier_semaphore()
        pl.semaphore_signal(barrier, inc=1, device_id=sibling, device_id_type=MESH)
        for k in range(1, chips):
            pl.semaphore_signal(barrier, inc=1, device_id={"batch": chip_up(k)}, device_id_type=MESH)
        for k in range(1, terms):
            pl.semaphore_signal(
                barrier, inc=1, device_id={"term": lax.rem(term + k, terms)}, device_id_type=MESH
            )
        pl.semaphore_wait(barrier, 1 + (chips - 1) + (terms - 1))
        score_all[term] = score_ref[...].astype(jnp.float32)
        for k in range(1, terms):
            score_copy(k).start()

    @pl.when(step < chunks)
    def _():
        c = step
        q_all[c, block] = impacts(q_in[...])
        for k in range(1, chips):
            q_to_chip(c, k).start()
        q_to_sibling(c).start()

    @pl.when(step == 0)
    def _():
        for k in range(1, terms):
            score_arrival(k).wait_recv()
        per = rows // score_all.shape[1]
        docs = score_all.shape[2]

        def score_block(at):
            return score_all[pl.ds(at * per, per)].reshape(rows, docs).astype(jnp.bfloat16)

        for k in range(chips):
            kept = chip_up(k) * 2
            score_keep_send[pl.ds(k * rows, rows), :] = score_block(kept + core)
            score_keep_send[pl.ds((chips + k) * rows, rows), :] = score_block(kept + other)
        ones = jnp.ones((16, docs), jnp.bfloat16)
        score_keep_send[pl.ds(2 * chips * rows, 16), :] = ones
        whole = score_all[...].reshape(2 * chips * rows, docs)
        score_t[pl.ds(0, docs), :] = whole.T.astype(jnp.bfloat16)
        score_t[pl.ds(docs, 16), :] = jnp.ones((16, 2 * chips * rows), jnp.bfloat16)
        for k in range(1, terms):
            score_copy(k).wait_send()

    @pl.when(step < chunks)
    def _():
        c = step
        half = chips * rows
        partial = jnp.dot(
            score_keep_send[...], impacts(d_in[...]), preferred_element_type=jnp.float32
        )
        width = partial.shape[1]
        p_send[c] = partial[half : 2 * half].astype(jnp.bfloat16).reshape(chips, rows, width)
        s_own[c] = partial[2 * half : 2 * half + 1]
        p_copy(c).start()
        s_copy(c).start()
        p_keep[c] = partial[:half].reshape(chips, rows, width)

    @pl.when(jnp.logical_and(step >= 1, step < chunks + 1))
    def _():
        c = step - 1
        p_copy(c).wait_recv()
        s_copy(c).wait_recv()
        for k in range(1, chips):
            x_send[c, k - 1] = (p_keep[c, k] + p_recv[c, k].astype(jnp.float32)).astype(jnp.bfloat16)
            x_copy(c, k).start()
        s_chip[c] = s_own[c] + s_recv[c]
        for k in range(1, chips):
            sx_copy(c, k).start()

    @pl.when(jnp.logical_and(step >= FORWARD_LAG, step < chunks + FORWARD_LAG))
    def _():
        c = step - FORWARD_LAG
        for k in range(1, chips):
            q_from_chip(c, k).wait_recv()
            q_forward(c, k).start()

    @pl.when(step >= OUT_LAG)
    def _():
        c = step - OUT_LAG
        q_from_sibling(c).wait_recv()
        for k in range(1, chips):
            q_forwarded(c, k).wait_recv()
        docs = d_in.shape[0]
        blocks = q_all.shape[1]
        width = q_all.shape[3]
        grads = jnp.dot(
            score_t[...], q_all[c].reshape(blocks * rows, width),
            preferred_element_type=jnp.float32,
        )
        for k in range(1, chips):
            x_copy(c, k).wait_recv()
            sx_copy(c, k).wait_recv()
        doc_sums = s_chip[c]
        for k in range(1, chips):
            doc_sums = doc_sums + s_far[c, k - 1]
        query_grad = p_keep[c, 0] + p_recv[c, 0].astype(jnp.float32)
        for k in range(1, chips):
            query_grad = query_grad + x_recv[c, k - 1].astype(jnp.float32)
        query_grad = query_grad + (2.0 * query_reg / num_queries) * grads[docs : docs + 1]
        q_out[...] = saturate_back(query_grad, q_again[...])
        doc_grad = grads[:docs] + (2.0 * doc_reg / num_docs) * doc_sums
        d_out[...] = saturate_back(doc_grad, d_again[...])
        q_to_sibling(c).wait_send()
        p_copy(c).wait_send()
        s_copy(c).wait_send()
        for k in range(1, chips):
            q_to_chip(c, k).wait_send()
            q_forward(c, k).wait_send()
            x_copy(c, k).wait_send()
            sx_copy(c, k).wait_send()


def on_device(chips, terms, query_logits, doc_logits, score_grad):
    rows, vocab = query_logits.shape
    docs = doc_logits.shape[0]
    score_rows = score_grad.shape[0]
    blocks = 2 * chips
    tiles = pl.cdiv(vocab, LANES)
    chunks = max(1, round(tiles / CHUNK_TILES))
    width = pl.cdiv(tiles, chunks) * LANES
    chunks = pl.cdiv(vocab, width)
    far = chips - 1

    def ahead(i):
        return 0, jnp.minimum(i, chunks - 1)

    def behind(i):
        return 0, jnp.maximum(i - OUT_LAG, 0)

    dma = pltpu.SemaphoreType.DMA
    scratch = [
        pltpu.VMEM((terms, score_rows, docs), jnp.float32),
        pltpu.VMEM((blocks * rows + 16, docs), jnp.bfloat16),
        pltpu.VMEM((docs + 16, blocks * rows), jnp.bfloat16),
        pltpu.VMEM((chunks, blocks, rows, width), jnp.bfloat16),
        pltpu.VMEM((chunks, chips, rows, width), jnp.float32),
        pltpu.VMEM((chunks, chips, rows, width), jnp.bfloat16),
        pltpu.VMEM((chunks, chips, rows, width), jnp.bfloat16),
        pltpu.VMEM((chunks, far, rows, width), jnp.bfloat16),
        pltpu.VMEM((chunks, far, rows, width), jnp.bfloat16),
        pltpu.VMEM((chunks, 1, width), jnp.float32),
        pltpu.VMEM((chunks, 1, width), jnp.float32),
        pltpu.VMEM((chunks, 1, width), jnp.float32),
        pltpu.VMEM((chunks, far, 1, width), jnp.float32),
        dma((terms - 1,)), dma((terms - 1,)),
        dma((chunks,)), dma((chunks,)),
        dma((chunks, far)), dma((chunks, far)),
        dma((chunks, far)), dma((chunks, far)),
        dma((chunks,)), dma((chunks,)),
        dma((chunks, far)), dma((chunks, far)),
        dma((chunks,)), dma((chunks,)),
        dma((chunks, far)), dma((chunks, far)),
    ]
    return pl.pallas_call(
        functools.partial(kernel, chips, terms, chunks, blocks * rows, blocks * docs),
        grid=(chunks + OUT_LAG,),
        out_shape=(
            jax.ShapeDtypeStruct(query_logits.shape, jnp.bfloat16),
            jax.ShapeDtypeStruct(doc_logits.shape, jnp.bfloat16),
        ),
        in_specs=[
            pl.BlockSpec((score_rows, docs), lambda i: (0, 0)),
            pl.BlockSpec((rows, width), ahead),
            pl.BlockSpec((docs, width), ahead),
            pl.BlockSpec((rows, width), behind),
            pl.BlockSpec((docs, width), behind),
        ],
        out_specs=(pl.BlockSpec((rows, width), behind), pl.BlockSpec((docs, width), behind)),
        scratch_shapes=scratch,
        compiler_params=pltpu.CompilerParams(
            collective_id=0,
            has_side_effects=True,
            vmem_limit_bytes=56 * 1024 * 1024,
            dimension_semantics=("arbitrary",),
        ),
        cost_estimate=pl.CostEstimate(
            flops=4 * docs * blocks * rows * vocab,
            bytes_accessed=6 * (rows + docs) * vocab,
            transcendentals=(rows + docs) * vocab,
        ),
    )(score_grad, query_logits, doc_logits, query_logits, doc_logits)


def solution(mesh):
    placed = (
        P(("grp", "batch", "sub"), "term"),
        P(("grp", "batch", "sub"), "term"),
        P(("grp", "term"), ("batch", "sub")),
    )
    return jax.shard_map(
        functools.partial(on_device, mesh.shape["batch"], mesh.shape["term"]),
        mesh=mesh,
        in_specs=placed,
        out_specs=(P(("grp", "batch", "sub"), "term"), P(("grp", "batch", "sub"), "term")),
        check_vma=False,
    )
```

time: 221 us -> 152 us (0.69)
  waiting for transfers between devices: 123 us -> 0 us
  Pallas kernels: 0 us -> 122 us
  matrix products: 34.1 us -> 0 us
  other arithmetic: 21.8 us -> 0 us
  local copies, waits for them, and re-layouts: 13 us -> 28.7 us
  blocking collectives: 15 us -> 0 us
  between operations: 13.8 us -> 0.65 us
    pallas_call x0 -> x1, Pallas kernels: none -> 122 us  [on_device(): pl.pallas_call(functools.partial(kernel, chips, terms, chunks, blocks * r...]
    reduce_scatter x1 -> x0, waiting for transfers between devices: 61.4 us -> none  [on_device(): lax.psum_scatter(jnp.dot(grad_rows, doc_impact, preferred_element_type=jn...]
    all_gather x1 -> x0, waiting for transfers between devices: 61 us -> none  [on_device(): lax.all_gather(query_impact, ('batch', 'sub'), axis=0, tiled=True)]
    dot_general x2 -> x0, matrix products: 34.1 us -> none  [the longest x1 21.5 us: on_device(): lax.dot_general(grad_rows, lax.all_gather(query_impact, ('batch', 'sub'),...]
    all_gather x1 -> x0, blocking collectives: 15 us -> none  [on_device(): score_cols = lax.all_gather(score_grad, 'term', axis=0, tiled=True)]
    pallas_call x0 -> x1, local copies, waits for them, and re-layouts: none -> 14.1 us  [on_device(): pl.pallas_call(functools.partial(kernel, chips, terms, chunks, blocks * r...]
    reduce_sum x1 -> x0, other arithmetic: 10.4 us -> none  [on_device(): jnp.sum(doc_impact, axis=0, dtype=jnp.float32)]
    convert_element_type x2 -> x0, other arithmetic: 10.4 us -> none  [the longest x1 5.72 us: impacts(): jnp.log1p(jnp.maximum(logits.astype(jnp.float32), 0.0)).astype(jnp.bfloat16)]
  transfers between devices with their start and end apart: 3 -> 0, of which waited for: 2 -> 0; matrix products, arithmetic and copies ran while one was open for 22% -> 0% of each run, Pallas kernels for 0% -> 0%
where the time goes in v1:
time: 152 us; the launch traced here: 151 us
  Pallas kernels  122 us (80%)
  local copies, waits for them, and re-layouts  28.7 us (19%)
    pallas_call x1, Pallas kernels, on_device(): pl.pallas_call(functools.partial(kernel, chips, terms, chunks, blocks * r...  122 us
    unnamed x4, local copies, waits for them, and re-layouts  14.6 us
    pallas_call x1, local copies, waits for them, and re-layouts, on_device(): pl.pallas_call(functools.partial(kernel, chips, terms, chunks, blocks * r...  14.1 us

profile of v1, /device:TPU:0, one launch (start us, length us, event | category | flops | bytes accessed | tf_op | source)
XLA Modules:
  0.0 151.3 jit_solution(12532072478249952323)
XLA Ops:
  0.6 13.2 %copy.5.d_in.d_again = bf16[128,37984]{1,0:T(8,128)(2,1)} copy(bf16[128,37984]{0,1:T(8,128)(2,1)} %param.4) | data formatting | bytes 19447808 | tf_op args[1]
  13.8 121.9 %shard_map.50 = (bf16[32,37984]{1,0:T(8,128)(2,1)}, bf16[128,37984]{1,0:T(8,128)(2,1)}) custom-call(bf16[32,128]{1,0:T(8,128)(2,1)} %score_ref.1, bf16[32,37984]{1,0:T(8,128)(2,1)} %q_again.1, bf16[128,37984]{1,0:T(8,128)(2,1)} %copy.5.d_in.d_again, bf16[32,37984]{1,0:T(8,128)(2,1)} %q_again.1, bf16[128,37984]{1,0:T(8,128)(2,1)} %copy.5.d_in.d_again), custom_call_target="tpu_custom_call" | custom-call | flops 2489319424 | bytes 36464640 | tf_op jit(solution)/shard_map/pallas_call | solution.py:277
  135.7 0.0 copy-start
  135.7 14.1 %copy.7 = bf16[128,37984]{0,1:T(8,128)(2,1)} copy(bf16[128,37984]{1,0:T(8,128)(2,1)} %get-tuple-element.3) | data formatting | bytes 19447808 | tf_op jit(solution)/shard_map/pallas_call | solution.py:277
  149.8 0.0 copy-done
  149.8 1.4 copy.9
Async XLA Ops:
  135.7 14.1 %copy-start = (bf16[32,37984]{1,0:T(8,128)(2,1)S(1)}, bf16[32,37984]{1,0:T(8,128)(2,1)}, u32[]{:S(2)}) copy-start(bf16[32,37984]{1,0:T(8,128)(2,1)} %get-tuple-element.6) | copy-start | bytes 7292932

commit v2 on v1

--- a/solution.py
+++ b/solution.py
@@ -30,7 +30,7 @@
 def kernel(
     chips, terms, chunks, num_queries, num_docs,
     score_ref, q_in, d_in, q_again, d_again, q_out, d_out,
-    score_all, score_keep_send, score_t,
+    score_all, score_keep_send, score_rows,
     q_all, p_keep, p_send, p_recv, x_send, x_recv, s_own, s_recv, s_chip, s_far,
     sc_ss, sc_rs, qs_ss, qs_rs, qx_ss, qx_rs, qf_ss, qf_rs,
     p_ss, p_rs, x_ss, x_rs, s_ss, s_rs, sx_ss, sx_rs,
@@ -159,8 +159,8 @@
         ones = jnp.ones((16, docs), jnp.bfloat16)
         score_keep_send[pl.ds(2 * chips * rows, 16), :] = ones
         whole = score_all[...].reshape(2 * chips * rows, docs)
-        score_t[pl.ds(0, docs), :] = whole.T.astype(jnp.bfloat16)
-        score_t[pl.ds(docs, 16), :] = jnp.ones((16, 2 * chips * rows), jnp.bfloat16)
+        score_rows[pl.ds(0, 2 * chips * rows), :] = whole.astype(jnp.bfloat16)
+        score_rows[pl.ds(2 * chips * rows, 16), :] = ones
         for k in range(1, terms):
             score_copy(k).wait_send()
 
@@ -168,8 +168,9 @@
     def _():
         c = step
         half = chips * rows
-        partial = jnp.dot(
-            score_keep_send[...], impacts(d_in[...]), preferred_element_type=jnp.float32
+        partial = lax.dot_general(
+            score_keep_send[...], impacts(d_in[...]), (((1,), (1,)), ((), ())),
+            preferred_element_type=jnp.float32,
         )
         width = partial.shape[1]
         p_send[c] = partial[half : 2 * half].astype(jnp.bfloat16).reshape(chips, rows, width)
@@ -203,13 +204,13 @@
         q_from_sibling(c).wait_recv()
         for k in range(1, chips):
             q_forwarded(c, k).wait_recv()
-        docs = d_in.shape[0]
         blocks = q_all.shape[1]
         width = q_all.shape[3]
-        grads = jnp.dot(
-            score_t[...], q_all[c].reshape(blocks * rows, width),
+        all_impacts = q_all[c].reshape(blocks * rows, width)
+        query_sums = jnp.dot(
+            jnp.ones((16, blocks * rows), jnp.bfloat16), all_impacts,
             preferred_element_type=jnp.float32,
-        )
+        )[:1]
         for k in range(1, chips):
             x_copy(c, k).wait_recv()
             sx_copy(c, k).wait_recv()
@@ -219,9 +220,20 @@
         query_grad = p_keep[c, 0] + p_recv[c, 0].astype(jnp.float32)
         for k in range(1, chips):
             query_grad = query_grad + x_recv[c, k - 1].astype(jnp.float32)
-        query_grad = query_grad + (2.0 * query_reg / num_queries) * grads[docs : docs + 1]
+        query_grad = query_grad + (2.0 * query_reg / num_queries) * query_sums
         q_out[...] = saturate_back(query_grad, q_again[...])
-        doc_grad = grads[:docs] + (2.0 * doc_reg / num_docs) * doc_sums
+        doc_reg_grad = (2.0 * doc_reg / num_docs) * doc_sums
+        high = doc_reg_grad.astype(jnp.bfloat16)
+        left = doc_reg_grad - high.astype(jnp.float32)
+        middle = left.astype(jnp.bfloat16)
+        low = (left - middle.astype(jnp.float32)).astype(jnp.bfloat16)
+        parts = jnp.concatenate(
+            [high, middle, low, jnp.zeros((13, width), jnp.bfloat16)], axis=0
+        )
+        doc_grad = lax.dot_general(
+            jnp.concatenate([all_impacts, parts], axis=0), score_rows[...],
+            (((0,), (0,)), ((), ())), preferred_element_type=jnp.float32,
+        )
         d_out[...] = saturate_back(doc_grad, d_again[...])
         q_to_sibling(c).wait_send()
         p_copy(c).wait_send()
@@ -236,6 +248,7 @@
 def on_device(chips, terms, query_logits, doc_logits, score_grad):
     rows, vocab = query_logits.shape
     docs = doc_logits.shape[0]
+    doc_logits = doc_logits.T
     score_rows = score_grad.shape[0]
     blocks = 2 * chips
     tiles = pl.cdiv(vocab, LANES)
@@ -250,11 +263,17 @@
     def behind(i):
         return 0, jnp.maximum(i - OUT_LAG, 0)
 
+    def ahead_docs(i):
+        return jnp.minimum(i, chunks - 1), 0
+
+    def behind_docs(i):
+        return jnp.maximum(i - OUT_LAG, 0), 0
+
     dma = pltpu.SemaphoreType.DMA
     scratch = [
         pltpu.VMEM((terms, score_rows, docs), jnp.float32),
         pltpu.VMEM((blocks * rows + 16, docs), jnp.bfloat16),
-        pltpu.VMEM((docs + 16, blocks * rows), jnp.bfloat16),
+        pltpu.VMEM((blocks * rows + 16, docs), jnp.bfloat16),
         pltpu.VMEM((chunks, blocks, rows, width), jnp.bfloat16),
         pltpu.VMEM((chunks, chips, rows, width), jnp.float32),
         pltpu.VMEM((chunks, chips, rows, width), jnp.bfloat16),
@@ -274,7 +293,7 @@
         dma((chunks,)), dma((chunks,)),
         dma((chunks, far)), dma((chunks, far)),
     ]
-    return pl.pallas_call(
+    query_grad, doc_grad = pl.pallas_call(
         functools.partial(kernel, chips, terms, chunks, blocks * rows, blocks * docs),
         grid=(chunks + OUT_LAG,),
         out_shape=(
@@ -284,11 +303,11 @@
         in_specs=[
             pl.BlockSpec((score_rows, docs), lambda i: (0, 0)),
             pl.BlockSpec((rows, width), ahead),
-            pl.BlockSpec((docs, width), ahead),
+            pl.BlockSpec((width, docs), ahead_docs),
             pl.BlockSpec((rows, width), behind),
-            pl.BlockSpec((docs, width), behind),
+            pl.BlockSpec((width, docs), behind_docs),
         ],
-        out_specs=(pl.BlockSpec((rows, width), behind), pl.BlockSpec((docs, width), behind)),
+        out_specs=(pl.BlockSpec((rows, width), behind), pl.BlockSpec((width, docs), behind_docs)),
         scratch_shapes=scratch,
         compiler_params=pltpu.CompilerParams(
             collective_id=0,
@@ -302,6 +321,7 @@
             transcendentals=(rows + docs) * vocab,
         ),
     )(score_grad, query_logits, doc_logits, query_logits, doc_logits)
+    return query_grad, doc_grad.T
 
 
 def solution(mesh):

time: 152 us -> 136 us (0.89)
  local copies, waits for them, and re-layouts: 28.7 us -> 12.6 us
    pallas_call x1 -> x0, local copies, waits for them, and re-layouts: 14.1 us -> none  [on_device(): pl.pallas_call(functools.partial(kernel, chips, terms, chunks, blocks * r...]
    unnamed x4 -> x2, local copies, waits for them, and re-layouts: 14.6 us -> 12.6 us
where the time goes in v2:
time: 136 us; the launch traced here: 135 us
  Pallas kernels  122 us (90%)
  local copies, waits for them, and re-layouts  12.6 us (9%)
    pallas_call x1, Pallas kernels, on_device(): pl.pallas_call(functools.partial(kernel, chips, terms, chunks, blocks * r...  122 us
    unnamed x2, local copies, waits for them, and re-layouts  12.6 us

profile of v2, /device:TPU:0, one launch (start us, length us, event | category | flops | bytes accessed | tf_op | source)
XLA Modules:
  0.0 135.2 jit_solution(4560928672423077628)
XLA Ops:
  0.6 122.0 %shard_map.50 = (bf16[32,37984]{1,0:T(8,128)(2,1)}, bf16[37984,128]{1,0:T(8,128)(2,1)}) custom-call(bf16[32,128]{1,0:T(8,128)(2,1)} %score_ref.1, bf16[32,37984]{1,0:T(8,128)(2,1)} %q_again.1, bf16[37984,128]{1,0:T(8,128)(2,1)} %bitcast.2, bf16[32,37984]{1,0:T(8,128)(2,1)} %q_again.1, bf16[37984,128]{1,0:T(8,128)(2,1)} %bitcast.3), custom_call_target="tpu_custom_call" | custom-call | flops 2489319424 | bytes 36464640 | tf_op jit(solution)/shard_map/pallas_call | solution.py:296
  122.7 3.3 %copy.7 = bf16[32,37984]{1,0:T(8,128)(2,1)} copy(bf16[32,37984]{1,0:T(8,128)(2,1)} %get-tuple-element.8) | data formatting | bytes 4861952
  126.0 9.3 %copy.8 = bf16[128,37984]{0,1:T(8,128)(2,1)} copy(bf16[128,37984]{0,1:T(8,128)(2,1)} %bitcast.4) | data formatting | bytes 19447808

commit v3 on v2

--- a/solution.py
+++ b/solution.py
@@ -34,6 +34,7 @@
     q_all, p_keep, p_send, p_recv, x_send, x_recv, s_own, s_recv, s_chip, s_far,
     sc_ss, sc_rs, qs_ss, qs_rs, qx_ss, qx_rs, qf_ss, qf_rs,
     p_ss, p_rs, x_ss, x_rs, s_ss, s_rs, sx_ss, sx_rs,
+    q_ring, d_ring, qw_sem, dw_sem,
 ):
     step = pl.program_id(0)
     rows = q_in.shape[0]
@@ -117,6 +118,18 @@
         return remote(
             s_chip.at[c], s_far.at[c, k - 1], sx_ss.at[c, k - 1], sx_rs.at[c, k - 1],
             {"batch": chip_up(k)},
+        )
+
+    width = q_in.shape[1]
+
+    def q_write(c):
+        slot = lax.rem(c, 2)
+        return pltpu.make_async_copy(q_ring.at[slot], q_out.at[c], qw_sem.at[slot])
+
+    def d_write(c):
+        slot = lax.rem(c, 2)
+        return pltpu.make_async_copy(
+            d_ring.at[slot], d_out.at[pl.ds(pl.multiple_of(c * width, LANES), width)], dw_sem.at[slot]
         )
 
     @pl.when(step == 0)
@@ -221,7 +234,14 @@
         for k in range(1, chips):
             query_grad = query_grad + x_recv[c, k - 1].astype(jnp.float32)
         query_grad = query_grad + (2.0 * query_reg / num_queries) * query_sums
-        q_out[...] = saturate_back(query_grad, q_again[...])
+        slot = lax.rem(c, 2)
+
+        @pl.when(c >= 2)
+        def _():
+            q_write(c - 2).wait()
+            d_write(c - 2).wait()
+
+        q_ring[slot] = saturate_back(query_grad, q_again[...])
         doc_reg_grad = (2.0 * doc_reg / num_docs) * doc_sums
         high = doc_reg_grad.astype(jnp.bfloat16)
         left = doc_reg_grad - high.astype(jnp.float32)
@@ -234,7 +254,9 @@
             jnp.concatenate([all_impacts, parts], axis=0), score_rows[...],
             (((0,), (0,)), ((), ())), preferred_element_type=jnp.float32,
         )
-        d_out[...] = saturate_back(doc_grad, d_again[...])
+        d_ring[slot] = saturate_back(doc_grad, d_again[...])
+        q_write(c).start()
+        d_write(c).start()
         q_to_sibling(c).wait_send()
         p_copy(c).wait_send()
         s_copy(c).wait_send()
@@ -243,6 +265,12 @@
             q_forward(c, k).wait_send()
             x_copy(c, k).wait_send()
             sx_copy(c, k).wait_send()
+
+        @pl.when(c == chunks - 1)
+        def _():
+            for last in range(max(0, chunks - 2), chunks):
+                q_write(last).wait()
+                d_write(last).wait()
 
 
 def on_device(chips, terms, query_logits, doc_logits, score_grad):
@@ -292,13 +320,16 @@
         dma((chunks, far)), dma((chunks, far)),
         dma((chunks,)), dma((chunks,)),
         dma((chunks, far)), dma((chunks, far)),
+        pltpu.VMEM((2, rows, width), jnp.bfloat16),
+        pltpu.VMEM((2, width, docs), jnp.bfloat16),
+        dma((2,)), dma((2,)),
     ]
     query_grad, doc_grad = pl.pallas_call(
         functools.partial(kernel, chips, terms, chunks, blocks * rows, blocks * docs),
         grid=(chunks + OUT_LAG,),
         out_shape=(
-            jax.ShapeDtypeStruct(query_logits.shape, jnp.bfloat16),
-            jax.ShapeDtypeStruct(doc_logits.shape, jnp.bfloat16),
+            pltpu.VMEM((chunks, rows, width), jnp.bfloat16),
+            pltpu.VMEM((chunks * width, docs), jnp.bfloat16),
         ),
         in_specs=[
             pl.BlockSpec((score_rows, docs), lambda i: (0, 0)),
@@ -307,12 +338,12 @@
             pl.BlockSpec((rows, width), behind),
             pl.BlockSpec((width, docs), behind_docs),
         ],
-        out_specs=(pl.BlockSpec((rows, width), behind), pl.BlockSpec((width, docs), behind_docs)),
+        out_specs=(pl.BlockSpec(memory_space=pl.ANY), pl.BlockSpec(memory_space=pl.ANY)),
         scratch_shapes=scratch,
         compiler_params=pltpu.CompilerParams(
             collective_id=0,
             has_side_effects=True,
-            vmem_limit_bytes=56 * 1024 * 1024,
+            vmem_limit_bytes=46 * 1024 * 1024,
             dimension_semantics=("arbitrary",),
         ),
         cost_estimate=pl.CostEstimate(
@@ -321,7 +352,8 @@
             transcendentals=(rows + docs) * vocab,
         ),
     )(score_grad, query_logits, doc_logits, query_logits, doc_logits)
-    return query_grad, doc_grad.T
+    query_grad = query_grad.transpose(1, 0, 2).reshape(rows, chunks * width)[:, :vocab]
+    return query_grad, doc_grad[:vocab].T
 
 
 def solution(mesh):

time: 136 us -> 128 us (0.941)
  local copies, waits for them, and re-layouts: 12.6 us -> 5.78 us
    unnamed x2 -> x0, local copies, waits for them, and re-layouts: 12.6 us -> none
    transpose x0 -> x1, local copies, waits for them, and re-layouts: none -> 4.17 us  [on_device(): return (query_grad, doc_grad[:vocab].T)]
    reshape x0 -> x1, local copies, waits for them, and re-layouts: none -> 1.61 us  [on_device(): query_grad.transpose(1, 0, 2).reshape(rows, chunks * width)[:, :vocab]]
where the time goes in v3:
time: 128 us
  Pallas kernels  122 us (95%)
  local copies, waits for them, and re-layouts  5.78 us (5%)
    pallas_call x1, Pallas kernels, on_device(): pl.pallas_call(functools.partial(kernel, chips, terms, chunks, blocks * r...  122 us
    transpose x1, local copies, waits for them, and re-layouts, on_device(): return (query_grad, doc_grad[:vocab].T)  4.17 us

profile of v3, /device:TPU:0, one launch (start us, length us, event | category | flops | bytes accessed | tf_op | source)
XLA Modules:
  0.0 127.9 jit_solution(9517397393672702694)
XLA Ops:
  0.6 121.5 %shard_map.50 = (bf16[27,32,1408]{2,1,0:T(8,128)(2,1)S(1)}, bf16[38016,128]{1,0:T(8,128)(2,1)S(1)}) custom-call(bf16[32,128]{1,0:T(8,128)(2,1)} %score_ref.1, bf16[32,37984]{1,0:T(8,128)(2,1)} %q_again.1, bf16[37984,128]{1,0:T(8,128)(2,1)} %bitcast.8, bf16[32,37984]{1,0:T(8,128)(2,1)} %q_again.1, bf16[37984,128]{1,0:T(8,128)(2,1)} %bitcast.9), custom_call_target="tpu_custom_call" | custom-call | flops 2489319424 | bytes 36464640 | tf_op jit(solution)/shard_map/pallas_call | solution.py:327
  122.1 1.6 %copy.6 = bf16[27,4,8,1408]{3,2,0,1:T(8,128)(2,1)} copy(bf16[27,4,8,1408]{3,2,1,0:T(8,128)(2,1)S(1)} %bitcast.7) | data formatting | bytes 4866048 | tf_op jit(solution)/shard_map/reshape | solution.py:355
  123.8 4.2 %slice_bitcast_fusion = bf16[128,37984]{0,1:T(8,128)(2,1)} fusion(bf16[38016,128]{1,0:T(8,128)(2,1)S(1)} %get-tuple-element.5), kind=kLoop, calls=%fused_computation | loop fusion | bytes 19447808 | tf_op jit(solution)/shard_map/transpose | solution.py:356

commit v4 on v3

--- a/solution.py
+++ b/solution.py
@@ -11,7 +11,7 @@
 doc_reg = 0.6
 
 LANES = 128
-CHUNK_TILES = 11
+CHUNK_TILES = 27
 FORWARD_LAG = 2
 OUT_LAG = 3
 MESH = pl.DeviceIdType.MESH
@@ -31,9 +31,9 @@
     chips, terms, chunks, num_queries, num_docs,
     score_ref, q_in, d_in, q_again, d_again, q_out, d_out,
     score_all, score_keep_send, score_rows,
-    q_all, p_keep, p_send, p_recv, x_send, x_recv, s_own, s_recv, s_chip, s_far,
+    q_all, p_keep, p_send, p_recv, x_send, x_recv, s_own, s_recv, s_chip, s_pack, s_far, s_rows,
     sc_ss, sc_rs, qs_ss, qs_rs, qx_ss, qx_rs, qf_ss, qf_rs,
-    p_ss, p_rs, x_ss, x_rs, s_ss, s_rs, sx_ss, sx_rs,
+    p_ss, p_rs, x_ss, x_rs, s_ss, s_rs, sx_ss, sx_rs, sf_ss, sf_rs,
     q_ring, d_ring, qw_sem, dw_sem,
 ):
     step = pl.program_id(0)
@@ -116,11 +116,25 @@
 
     def sx_copy(c, k):
         return remote(
-            s_chip.at[c], s_far.at[c, k - 1], sx_ss.at[c, k - 1], sx_rs.at[c, k - 1],
+            s_pack.at[c, core], s_far.at[c, k - 1, core], sx_ss.at[c, k - 1], sx_rs.at[c, k - 1],
             {"batch": chip_up(k)},
         )
 
+    def s_forward(c, k):
+        return remote(
+            s_far.at[c, k - 1, core], s_far.at[c, k - 1, core],
+            sf_ss.at[c, k - 1], sf_rs.at[c, k - 1], sibling,
+        )
+
+    def s_forwarded(c, k):
+        return remote(
+            s_far.at[c, k - 1, other], s_far.at[c, k - 1, other],
+            sf_ss.at[c, k - 1], sf_rs.at[c, k - 1], sibling,
+        )
+
     width = q_in.shape[1]
+    tiles = width // LANES
+    half_tiles = pl.cdiv(tiles, 2)
 
     def q_write(c):
         slot = lax.rem(c, 2)
@@ -143,6 +157,7 @@
                 barrier, inc=1, device_id={"term": lax.rem(term + k, terms)}, device_id_type=MESH
             )
         pl.semaphore_wait(barrier, 1 + (chips - 1) + (terms - 1))
+        s_rows[...] = jnp.zeros_like(s_rows)
         score_all[term] = score_ref[...].astype(jnp.float32)
         for k in range(1, terms):
             score_copy(k).start()
@@ -197,12 +212,17 @@
         c = step - 1
         p_copy(c).wait_recv()
         s_copy(c).wait_recv()
+        chip_sums = s_own[c] + s_recv[c]
+        s_chip[c] = chip_sums
+        for t in range(tiles):
+            h, r = divmod(t, half_tiles)
+            s_rows[h, r : r + 1, :] = chip_sums[:, t * LANES : (t + 1) * LANES]
+        s_pack[c] = s_rows[...].astype(jnp.bfloat16)
+        for k in range(1, chips):
+            sx_copy(c, k).start()
         for k in range(1, chips):
             x_send[c, k - 1] = (p_keep[c, k] + p_recv[c, k].astype(jnp.float32)).astype(jnp.bfloat16)
             x_copy(c, k).start()
-        s_chip[c] = s_own[c] + s_recv[c]
-        for k in range(1, chips):
-            sx_copy(c, k).start()
 
     @pl.when(jnp.logical_and(step >= FORWARD_LAG, step < chunks + FORWARD_LAG))
     def _():
@@ -210,6 +230,8 @@
         for k in range(1, chips):
             q_from_chip(c, k).wait_recv()
             q_forward(c, k).start()
+            sx_copy(c, k).wait_recv()
+            s_forward(c, k).start()
 
     @pl.when(step >= OUT_LAG)
     def _():
@@ -224,16 +246,15 @@
             jnp.ones((16, blocks * rows), jnp.bfloat16), all_impacts,
             preferred_element_type=jnp.float32,
         )[:1]
-        for k in range(1, chips):
-            x_copy(c, k).wait_recv()
-            sx_copy(c, k).wait_recv()
         doc_sums = s_chip[c]
         for k in range(1, chips):
-            doc_sums = doc_sums + s_far[c, k - 1]
-        query_grad = p_keep[c, 0] + p_recv[c, 0].astype(jnp.float32)
-        for k in range(1, chips):
-            query_grad = query_grad + x_recv[c, k - 1].astype(jnp.float32)
-        query_grad = query_grad + (2.0 * query_reg / num_queries) * query_sums
+            s_forwarded(c, k).wait_recv()
+            s_rows[...] = s_far[c, k - 1].astype(jnp.float32)
+            pieces = []
+            for t in range(tiles):
+                h, r = divmod(t, half_tiles)
+                pieces.append(s_rows[h, r : r + 1, :])
+            doc_sums = doc_sums + jnp.concatenate(pieces, axis=1)
         slot = lax.rem(c, 2)
 
         @pl.when(c >= 2)
@@ -241,7 +262,6 @@
             q_write(c - 2).wait()
             d_write(c - 2).wait()
 
-        q_ring[slot] = saturate_back(query_grad, q_again[...])
         doc_reg_grad = (2.0 * doc_reg / num_docs) * doc_sums
         high = doc_reg_grad.astype(jnp.bfloat16)
         left = doc_reg_grad - high.astype(jnp.float32)
@@ -255,8 +275,14 @@
             (((0,), (0,)), ((), ())), preferred_element_type=jnp.float32,
         )
         d_ring[slot] = saturate_back(doc_grad, d_again[...])
+        d_write(c).start()
+        query_grad = p_keep[c, 0] + p_recv[c, 0].astype(jnp.float32)
+        query_grad = query_grad + (2.0 * query_reg / num_queries) * query_sums
+        for k in range(1, chips):
+            x_copy(c, k).wait_recv()
+            query_grad = query_grad + x_recv[c, k - 1].astype(jnp.float32)
+        q_ring[slot] = saturate_back(query_grad, q_again[...])
         q_write(c).start()
-        d_write(c).start()
         q_to_sibling(c).wait_send()
         p_copy(c).wait_send()
         s_copy(c).wait_send()
@@ -265,6 +291,7 @@
             q_forward(c, k).wait_send()
             x_copy(c, k).wait_send()
             sx_copy(c, k).wait_send()
+            s_forward(c, k).wait_send()
 
         @pl.when(c == chunks - 1)
         def _():
@@ -284,6 +311,7 @@
     width = pl.cdiv(tiles, chunks) * LANES
     chunks = pl.cdiv(vocab, width)
     far = chips - 1
+    half_rows = pl.cdiv(pl.cdiv(width // LANES, 2), 16) * 16
 
     def ahead(i):
         return 0, jnp.minimum(i, chunks - 1)
@@ -311,7 +339,9 @@
         pltpu.VMEM((chunks, 1, width), jnp.float32),
         pltpu.VMEM((chunks, 1, width), jnp.float32),
         pltpu.VMEM((chunks, 1, width), jnp.float32),
-        pltpu.VMEM((chunks, far, 1, width), jnp.float32),
+        pltpu.VMEM((chunks, 2, half_rows, LANES), jnp.bfloat16),
+        pltpu.VMEM((chunks, far, 2, half_rows, LANES), jnp.bfloat16),
+        pltpu.VMEM((2, half_rows, LANES), jnp.float32),
         dma((terms - 1,)), dma((terms - 1,)),
         dma((chunks,)), dma((chunks,)),
         dma((chunks, far)), dma((chunks, far)),
@@ -319,6 +349,7 @@
         dma((chunks,)), dma((chunks,)),
         dma((chunks, far)), dma((chunks, far)),
         dma((chunks,)), dma((chunks,)),
+        dma((chunks, far)), dma((chunks, far)),
         dma((chunks, far)), dma((chunks, far)),
         pltpu.VMEM((2, rows, width), jnp.bfloat16),
         pltpu.VMEM((2, width, docs), jnp.bfloat16),

time: 128 us -> 123 us (0.961)
  Pallas kernels: 122 us -> 116 us
    pallas_call x1, Pallas kernels: 122 us -> 116 us  [on_device(): pl.pallas_call(functools.partial(kernel, chips, terms, chunks, blocks * r...]
where the time goes in v4:
time: 123 us
  Pallas kernels  116 us (94%)
  local copies, waits for them, and re-layouts  5.77 us (5%)
    pallas_call x1, Pallas kernels, on_device(): pl.pallas_call(functools.partial(kernel, chips, terms, chunks, blocks * r...  116 us
    transpose x1, local copies, waits for them, and re-layouts, on_device(): return (query_grad, doc_grad[:vocab].T)  4.17 us

profile of v4, /device:TPU:0, one launch (start us, length us, event | category | flops | bytes accessed | tf_op | source)
XLA Modules:
  0.0 122.8 jit_solution(5188322282397322979)
XLA Ops:
  0.6 116.4 %shard_map.50 = (bf16[11,32,3456]{2,1,0:T(8,128)(2,1)S(1)}, bf16[38016,128]{1,0:T(8,128)(2,1)S(1)}) custom-call(bf16[32,128]{1,0:T(8,128)(2,1)} %score_ref.1, bf16[32,37984]{1,0:T(8,128)(2,1)} %q_again.1, bf16[37984,128]{1,0:T(8,128)(2,1)} %bitcast.8, bf16[32,37984]{1,0:T(8,128)(2,1)} %q_again.1, bf16[37984,128]{1,0:T(8,128)(2,1)} %bitcast.9), custom_call_target="tpu_custom_call" | custom-call | flops 2489319424 | bytes 36464640 | tf_op jit(solution)/shard_map/pallas_call | solution.py:358
  117.0 1.6 %copy.6 = bf16[11,4,8,3456]{3,2,0,1:T(8,128)(2,1)} copy(bf16[11,4,8,3456]{3,2,1,0:T(8,128)(2,1)S(1)} %bitcast.7) | data formatting | bytes 4866048 | tf_op jit(solution)/shard_map/reshape | solution.py:386
  118.6 4.2 %slice_bitcast_fusion = bf16[128,37984]{0,1:T(8,128)(2,1)} fusion(bf16[38016,128]{1,0:T(8,128)(2,1)S(1)} %get-tuple-element.5), kind=kLoop, calls=%fused_computation | loop fusion | bytes 19447808 | tf_op jit(solution)/shard_map/transpose | solution.py:387

commit v5 on v4

--- a/solution.py
+++ b/solution.py
@@ -298,6 +298,20 @@
             for last in range(max(0, chunks - 2), chunks):
                 q_write(last).wait()
                 d_write(last).wait()
+
+
+def drain(width, d_from, d_to, d_sem):
+    vocab = d_to.shape[0]
+    chunks = pl.cdiv(vocab, width)
+    copies = []
+    for c in range(chunks):
+        size = min(width, vocab - c * width)
+        part = pl.ds(c * width, size)
+        copies.append(pltpu.make_async_copy(d_from.at[part], d_to.at[part], d_sem.at[c]))
+    for copy in copies:
+        copy.start()
+    for copy in copies:
+        copy.wait()
 
 
 def on_device(chips, terms, query_logits, doc_logits, score_grad):
@@ -384,7 +398,15 @@
         ),
     )(score_grad, query_logits, doc_logits, query_logits, doc_logits)
     query_grad = query_grad.transpose(1, 0, 2).reshape(rows, chunks * width)[:, :vocab]
-    return query_grad, doc_grad[:vocab].T
+    doc_grad = pl.pallas_call(
+        functools.partial(drain, width),
+        out_shape=jax.ShapeDtypeStruct((vocab, docs), jnp.bfloat16),
+        in_specs=[pl.BlockSpec(memory_space=pl.ANY)],
+        out_specs=pl.BlockSpec(memory_space=pl.ANY),
+        scratch_shapes=[dma((chunks,))],
+        compiler_params=pltpu.CompilerParams(vmem_limit_bytes=4 * 1024 * 1024),
+    )(doc_grad)
+    return query_grad, doc_grad.T
 
 
 def solution(mesh):

time: 123 us -> 123 us (level)
  local copies, waits for them, and re-layouts: 5.77 us -> 1.6 us
  Pallas kernels: 116 us -> 120 us
    transpose x1 -> x0, local copies, waits for them, and re-layouts: 4.17 us -> none  [on_device(): return (query_grad, doc_grad[:vocab].T)]
    pallas_call x0 -> x1, Pallas kernels: none -> 3.79 us  [on_device(): pl.pallas_call(functools.partial(drain, width), out_shape=jax.ShapeDtypeS...]
where the time goes in v5:
time: 123 us; the launch traced here: 122 us
  Pallas kernels  120 us (98%)
  local copies, waits for them, and re-layouts  1.6 us (1%)
    pallas_call x1, Pallas kernels, on_device(): pl.pallas_call(functools.partial(kernel, chips, terms, chunks, blocks * r...  116 us
    pallas_call x1, Pallas kernels, on_device(): pl.pallas_call(functools.partial(drain, width), out_shape=jax.ShapeDtypeS...  3.79 us

profile of v5, /device:TPU:0, one launch (start us, length us, event | category | flops | bytes accessed | tf_op | source)
XLA Modules:
  0.0 122.4 jit_solution(9080539564637271152)
XLA Ops:
  0.6 116.4 %shard_map.50 = (bf16[11,32,3456]{2,1,0:T(8,128)(2,1)S(1)}, bf16[38016,128]{1,0:T(8,128)(2,1)S(1)}) custom-call(bf16[32,128]{1,0:T(8,128)(2,1)} %score_ref.1, bf16[32,37984]{1,0:T(8,128)(2,1)} %q_again.1, bf16[37984,128]{1,0:T(8,128)(2,1)} %bitcast.7, bf16[32,37984]{1,0:T(8,128)(2,1)} %q_again.1, bf16[37984,128]{1,0:T(8,128)(2,1)} %bitcast.8), custom_call_target="tpu_custom_call" | custom-call | flops 2489319424 | bytes 36464640 | tf_op jit(solution)/shard_map/pallas_call | solution.py:372
  117.0 1.6 %copy.6 = bf16[11,4,8,3456]{3,2,0,1:T(8,128)(2,1)} copy(bf16[11,4,8,3456]{3,2,1,0:T(8,128)(2,1)S(1)} %bitcast.6) | data formatting | bytes 4866048 | tf_op jit(solution)/shard_map/reshape | solution.py:400
  118.6 3.8 %shard_map.51 = bf16[37984,128]{1,0:T(8,128)(2,1)} custom-call(bf16[38016,128]{1,0:T(8,128)(2,1)S(1)} %get-tuple-element.5.d_from), custom_call_target="tpu_custom_call" | custom-call | tf_op jit(solution)/shard_map/pallas_call | solution.py:401
